TPU v7x, 512 devices: a whole 4x4x16 slice. The times are simulated.
512 devices in a mesh: dp: 16 (over x, y), expert: 32 (over z, core).
Axes of the slice: x: 4, y: 4, z: 16, core: 2. Of those that a mesh axis runs over, the one named last changes fastest.
Arguments:
- tokens: bfloat16 [4096, 4096], P('expert', 'dp'), may hold values from -6 to 6
- expert_ids: int32 [4096, 8], P('expert'), may hold values from 0 to 127, all different within a row; in each aligned block of 128 rows (0 to 127, 128 to 255, ...) at most 12 rows name the same one
- gate_codes: int32 [4096, 8], P('expert'), may hold values from 1 to 255
- out_grad: bfloat16 [4096, 4096], P('expert', 'dp'), may hold values from -3 to 3
- w_in: bfloat16 [32, 4096, 3072], P('expert', 'dp'), may hold values from -0.09375 to 0.09375
- w_out: bfloat16 [32, 1536, 4096], P('expert', None, 'dp'), may hold values from -0.625 to 0.625
Outputs:
- output: bfloat16 [4096, 4096], P('expert', 'dp')
- token_grad: bfloat16 [4096, 4096], P('expert', 'dp')
- w_in_grad: bfloat16 [32, 4096, 3072], P('expert', 'dp')
- w_out_grad: bfloat16 [32, 1536, 4096], P('expert', None, 'dp')
Inputs may be any that keep to these rules, and one draw needn't show every extreme that they name: `expert_ids`: each token names 8 different experts. Among the 128 tokens of one index of the expert axis (aligned blocks of tokens) no expert is named by more than 12 tokens, a bound that some block reaches.
All inputs are finite; a program needn't handle non-finite values.
Results may differ from a plain program's by a relative error of at most 0.029.
Values may be sent and summed in bfloat16 or wider, within the bound.
A program may use at most 64 MiB of HBM per device.

v0:
```python
import jax
import jax.numpy as jnp
from jax import lax
from jax.sharding import PartitionSpec as P

ALL_EXP = 128


def activation(values):
    sigma = jax.nn.sigmoid(values)
    return (values * sigma, sigma * (1.0 + values * (1.0 - sigma)))


def body(tokens, expert_ids, gate_codes, out_grad, w_in, w_out):
    expert_devices = lax.axis_size("expert")
    local_experts = w_in.shape[0]
    window = local_experts * expert_devices
    token_count = tokens.shape[0]
    slice_width = tokens.shape[1]
    top_count = expert_ids.shape[1]
    hidden_units = w_out.shape[1]
    capacity = 3 * token_count * top_count // (2 * ALL_EXP)
    rows_total = capacity * expert_devices
    code_values = gate_codes.astype(jnp.float32)
    shares = code_values / jnp.sum(code_values, axis=1, keepdims=True)
    matches = (expert_ids[:, :, None] == jnp.arange(window, dtype=jnp.int32)[None, None, :]).astype(
        jnp.float32
    )
    chosen = jnp.sum(matches, axis=1)
    weight_of = jnp.sum(shares[:, :, None] * matches, axis=1)
    lower = (jnp.arange(token_count)[:, None] > jnp.arange(token_count)[None, :]).astype(
        jnp.bfloat16
    )
    positions = jnp.dot(lower, chosen.astype(jnp.bfloat16), preferred_element_type=jnp.float32)
    targets = jnp.arange(capacity, dtype=jnp.float32)
    placer = jnp.transpose(chosen)[:, None, :] * (
        jnp.transpose(positions)[:, None, :] == targets[None, :, None]
    )
    placer = jnp.transpose(
        placer.reshape(expert_devices, local_experts, capacity, token_count), (1, 0, 2, 3)
    )
    weight_rows = jnp.transpose(
        jnp.transpose(weight_of).reshape(expert_devices, local_experts, token_count), (1, 0, 2)
    )
    slot_weight = jnp.sum(placer * weight_rows[:, :, None, :], axis=3)
    combine = placer * slot_weight[:, :, :, None]
    placer_half = placer.astype(jnp.bfloat16)

    def pack_rows(rows):
        return jnp.einsum(
            "lect,td->lecd", placer_half, rows, preferred_element_type=jnp.float32
        ).astype(jnp.bfloat16)

    def unpack_rows(results):
        shaped = results.reshape(local_experts, expert_devices, capacity, slice_width)
        return lax.all_to_all(shaped, "expert", split_axis=1, concat_axis=1, tiled=True)

    packed = pack_rows(tokens)
    arrived = lax.all_to_all(packed, "expert", split_axis=1, concat_axis=1, tiled=True)
    input_rows = arrived.reshape(local_experts, rows_total, slice_width)
    partial_value = jnp.einsum("lrd,ldf->lrf", input_rows, w_in, preferred_element_type=jnp.float32)
    partial_value = partial_value.reshape(local_experts, rows_total, 2, hidden_units)
    summed = lax.psum_scatter(
        partial_value.astype(jnp.bfloat16), "dp", scatter_dimension=3, tiled=True
    ).astype(jnp.float32)
    gate_pre = summed[:, :, 0]
    up_pre = summed[:, :, 1]
    active, slopes = activation(gate_pre)
    hidden = lax.all_gather((active * up_pre).astype(jnp.bfloat16), "dp", axis=2, tiled=True)
    expert_out = jnp.einsum(
        "lrf,lfd->lrd", hidden, w_out, preferred_element_type=jnp.float32
    ).astype(jnp.bfloat16)
    returned_out = unpack_rows(expert_out)
    output = jnp.einsum(
        "lect,lecd->td", combine, returned_out.astype(jnp.float32), precision=lax.Precision.HIGHEST
    ).astype(jnp.bfloat16)
    packed_grad = pack_rows(out_grad)
    route_grad = (slot_weight[:, :, :, None] * packed_grad.astype(jnp.float32)).astype(jnp.bfloat16)
    grad_arrived = lax.all_to_all(route_grad, "expert", split_axis=1, concat_axis=1, tiled=True)
    grad_rows = grad_arrived.reshape(local_experts, rows_total, slice_width)
    w_out_grad = jnp.einsum(
        "lrf,lrd->lfd", hidden, grad_rows, preferred_element_type=jnp.float32
    ).astype(jnp.bfloat16)
    hidden_partial = jnp.einsum(
        "lrd,lfd->lrf", grad_rows, w_out, preferred_element_type=jnp.float32
    )
    w_in_split = w_in.reshape(local_experts, slice_width, 2, hidden_units)
    hidden_grad = lax.psum_scatter(
        hidden_partial.astype(jnp.bfloat16), "dp", scatter_dimension=2, tiled=True
    ).astype(jnp.float32)
    unit_share = jnp.stack([hidden_grad * up_pre * slopes, hidden_grad * active], axis=2).astype(
        jnp.bfloat16
    )
    segment = lax.all_gather(unit_share, "dp", axis=3, tiled=True)
    input_acc = jnp.einsum(
        "lrgf,ldgf->lrd", segment, w_in_split, preferred_element_type=jnp.float32
    )
    weight_part = jnp.einsum(
        "lrd,lrgf->ldgf", input_rows, segment, preferred_element_type=jnp.float32
    )
    w_in_grad = weight_part.reshape(local_experts, slice_width, 2 * hidden_units).astype(
        jnp.bfloat16
    )
    returned_grad = unpack_rows(input_acc.astype(jnp.bfloat16))
    token_grad = jnp.einsum(
        "lect,lecd->td", placer_half, returned_grad, preferred_element_type=jnp.float32
    ).astype(jnp.bfloat16)
    return (output, token_grad, w_in_grad, w_out_grad)


def solution(mesh):
    placed = (
        P("expert", "dp"),
        P("expert", None),
        P("expert", None),
        P("expert", "dp"),
        P("expert", "dp", None),
        P("expert", None, "dp"),
    )
    return jax.shard_map(
        body,
        mesh=mesh,
        in_specs=placed,
        out_specs=(
            P("expert", "dp"),
            P("expert", "dp"),
            P("expert", "dp", None),
            P("expert", None, "dp"),
        ),
        check_vma=False,
    )
```

profile of v0, /device:TPU:1, one launch (start us, length us, event | category | flops | bytes accessed | tf_op | source)
XLA Modules:
  0.0 444.7 jit_solution(12428511504532385068)
XLA Ops:
  7.2 0.8 convert_reduce_fusion.1
  9.5 1.0 fusion.27
  10.6 0.8 copy.44
  11.4 16.8 %all-to-all-start = ((bf16[1,32,12,256]{3,2,0,1:T(8,128)(2,1)}), bf16[1,32,12,256]{3,2,0,1:T(8,128)(2,1)S(1)}, u32[]{:S(2)}, u32[]{:S(2)}) async-start(bf16[1,32,12,256]{3,2,0,1:T(8,128)(2,1)} %copy.44), calls=%async_computation | async-start | bytes 524288 | tf_op jit(solution)/shard_map/all_to_all | solution.py:59
  28.2 2.6 copy.61
  30.8 19.4 %all-to-all-done = bf16[1,32,12,256]{3,2,0,1:T(8,128)(2,1)S(1)} async-done(((bf16[1,32,12,256]{3,2,0,1:T(8,128)(2,1)}), bf16[1,32,12,256]{3,2,0,1:T(8,128)(2,1)S(1)}, u32[]{:S(2)}, u32[]{:S(2)}) %all-to-all-start) | async-done | bytes 196640 | tf_op jit(solution)/shard_map/all_to_all | solution.py:59
  50.9 2.3 fusion.1
  53.2 4.6 %copy.46 = bf16[1,384,2,1536]{1,2,0,3:T(2,128)(2,1)} copy(bf16[1,384,2,1536]{3,1,2,0:T(8,128)(2,1)S(1)} %fusion.1) | data formatting | bytes 4718592 | tf_op jit(solution)/shard_map/convert_element_type | solution.py:64
  59.0 25.6 %all_to_all.20 = bf16[1,32,12,256]{3,2,0,1:T(8,128)(2,1)S(1)} all-to-all(bf16[1,32,12,256]{3,2,0,1:T(8,128)(2,1)S(1)} %copy.51), channel_id=1, replica_groups=mesh['dp'=16,'expert'=32] {'expert'}, dimensions={1} | all-to-all | bytes 393216 | tf_op jit(solution)/shard_map/all_to_all | solution.py:79
  85.4 1.5 fusion.2
  86.9 6.3 %copy.63 = bf16[1,384,1536]{1,0,2:T(2,128)(2,1)S(1)} copy(bf16[1,384,1536]{2,1,0:T(8,128)(2,1)} %fusion.2) | data formatting | bytes 2359296
  93.2 1.2 copy.106
  94.5 1.3 dynamic-slice
  96.4 74.9 %all-reduce.3.cloned.1.call-done = bf16[1,384,2,1536]{1,2,0,3:T(2,128)(2,1)} async-done(((bf16[1,384,2,1536]{1,2,0,3:T(2,128)(2,1)}), bf16[1,384,2,1536]{1,2,0,3:T(2,128)(2,1)}) %all-reduce.3.cloned.1.call-update) | async-done | bytes 2359312
  171.3 1.0 dynamic-slice_convert_fusion
  172.6 91.0 %reduce-scatter.4.cloned.1.call-done = bf16[96,384]{1,0:T(8,128)(2,1)} async-done(((bf16[1536,384]{1,0:T(8,128)(2,1)}), bf16[96,384]{1,0:T(8,128)(2,1)}) %reduce-scatter.4.cloned.1.call-update) | async-done | bytes 73744
  263.5 1.0 reshape_bitcast_fusion
  265.7 0.8 copy.55
  266.5 59.7 %all-gather.3.cloned.1.call-done = bf16[1,384,1536]{1,2,0:T(8,128)(2,1)} async-done(((bf16[1,384,96]{1,2,0:T(8,128)(2,1)}), bf16[1,384,1536]{1,2,0:T(8,128)(2,1)}) %all-gather.3.cloned.1.call-update) | async-done | bytes 1179664 | tf_op jit(solution)/shard_map/all_gather | solution.py:69
  326.2 1.8 fusion.15
  328.8 13.9 %all-to-all-start.1 = ((bf16[1,32,12,256]{3,2,0,1:T(8,128)(2,1)}), bf16[1,32,12,256]{3,2,0,1:T(8,128)(2,1)}, u32[]{:S(2)}, u32[]{:S(2)}) async-start(bf16[1,32,12,256]{3,2,0,1:T(8,128)(2,1)} %bitcast.12), calls=%async_computation.1 | async-start | bytes 524288 | tf_op jit(solution)/shard_map/all_to_all | solution.py:56
  342.7 2.1 reshape.260
  344.8 45.3 %all-gather.5.cloned.1.call-done = bf16[1,384,2,1536]{1,2,0,3:T(2,128)(2,1)} async-done(((bf16[1,384,2,96]{1,2,0,3:T(2,128)(2,1)}), bf16[1,384,2,1536]{1,2,0,3:T(2,128)(2,1)}) %all-gather.5.cloned.1.call-update) | async-done | bytes 2359312 | tf_op jit(solution)/shard_map/all_gather | solution.py:94
  390.0 5.6 %copy.56 = bf16[1,384,2,1536]{3,1,2,0:T(8,128)(2,1)S(1)} copy(bf16[1,384,2,1536]{1,2,0,3:T(2,128)(2,1)} %all-gather.5.cloned.1.call-done) | data formatting | bytes 4718592 | tf_op jit(solution)/shard_map/all_gather | solution.py:94
  395.7 2.9 fusion.18
  398.6 1.7 reshape.261
  400.2 14.1 %all-to-all-start.3 = ((bf16[1,32,12,256]{3,2,0,1:T(8,128)(2,1)}), bf16[1,32,12,256]{3,2,0,1:T(8,128)(2,1)}, u32[]{:S(2)}, u32[]{:S(2)}) async-start(bf16[1,32,12,256]{3,2,0,1:T(8,128)(2,1)} %bitcast.21), calls=%async_computation.3 | async-start | bytes 524288 | tf_op jit(solution)/shard_map/all_to_all | solution.py:56
  415.1 2.8 fusion.3
  417.8 2.0 fusion.29
  420.8 2.2 fusion
  423.0 13.4 %all-to-all-done.3 = bf16[1,32,12,256]{3,2,0,1:T(8,128)(2,1)} async-done(((bf16[1,32,12,256]{3,2,0,1:T(8,128)(2,1)}), bf16[1,32,12,256]{3,2,0,1:T(8,128)(2,1)}, u32[]{:S(2)}, u32[]{:S(2)}) %all-to-all-start.3) | async-done | bytes 196640 | tf_op jit(solution)/shard_map/all_to_all | solution.py:56
  436.4 1.8 fusion.28
  (38 shorter events, 8.0 us)
Async XLA Ops:
  7.2 78.2 %copy-start = (bf16[1,1536,256]{2,1,0:T(8,128)(2,1)S(1)}, bf16[1,1536,256]{2,1,0:T(8,128)(2,1)}, u32[]{:S(2)}) copy-start(bf16[1,1536,256]{2,1,0:T(8,128)(2,1)} %param.11) | copy-start | bytes 2359300
  11.4 38.8 %all-to-all-start = ((bf16[1,32,12,256]{3,2,0,1:T(8,128)(2,1)}), bf16[1,32,12,256]{3,2,0,1:T(8,128)(2,1)S(1)}, u32[]{:S(2)}, u32[]{:S(2)}) async-start(bf16[1,32,12,256]{3,2,0,1:T(8,128)(2,1)} %copy.44), calls=%async_computation | async-start | bytes 524288 | tf_op jit(solution)/shard_map/all_to_all | solution.py:59
  28.1 143.2 %all-reduce.3.cloned.1.call-start = ((), (), s32[]{:S(2)}) async-start(), calls=%async_computation.8 | async-start | bytes 4718592
  57.8 0.8 copy-start.5
  57.9 205.6 %reduce-scatter.4.cloned.1.call-start = ((), (), s32[]{:S(2)}) async-start(), calls=%async_computation.7 | async-start | bytes 1253376
  84.7 0.7 copy-start.3
  94.4 231.8 %all-gather.3.cloned.1.call-start = ((), (), s32[]{:S(2)}) async-start(), calls=%async_computation.5 | async-start | bytes 1253376 | tf_op jit(solution)/shard_map/all_gather | solution.py:69
  265.2 124.8 %all-gather.5.cloned.1.call-start = ((), (), s32[]{:S(2)}) async-start(), calls=%async_computation.6 | async-start | bytes 2506752 | tf_op jit(solution)/shard_map/all_gather | solution.py:94
  266.5 76.2 %copy-start.2 = (bf16[1,256,3072]{2,1,0:T(8,128)(2,1)S(1)}, bf16[1,256,3072]{2,1,0:T(8,128)(2,1)}, u32[]{:S(2)}) copy-start(bf16[1,256,3072]{2,1,0:T(8,128)(2,1)} %param.10) | copy-start | bytes 4718596
  328.8 71.5 %all-to-all-start.1 = ((bf16[1,32,12,256]{3,2,0,1:T(8,128)(2,1)}), bf16[1,32,12,256]{3,2,0,1:T(8,128)(2,1)}, u32[]{:S(2)}, u32[]{:S(2)}) async-start(bf16[1,32,12,256]{3,2,0,1:T(8,128)(2,1)} %bitcast.12), calls=%async_computation.1 | async-start | bytes 524288 | tf_op jit(solution)/shard_map/all_to_all | solution.py:56
  400.2 36.2 %all-to-all-start.3 = ((bf16[1,32,12,256]{3,2,0,1:T(8,128)(2,1)}), bf16[1,32,12,256]{3,2,0,1:T(8,128)(2,1)}, u32[]{:S(2)}, u32[]{:S(2)}) async-start(bf16[1,32,12,256]{3,2,0,1:T(8,128)(2,1)} %bitcast.21), calls=%async_computation.3 | async-start | bytes 524288 | tf_op jit(solution)/shard_map/all_to_all | solution.py:56
  414.3 5.5 %copy-start.1 = (bf16[1,384,2,1536]{1,2,0,3:T(2,128)(2,1)S(1)}, bf16[1,384,2,1536]{1,2,0,3:T(2,128)(2,1)}, u32[]{:S(2)}) copy-start(bf16[1,384,2,1536]{1,2,0,3:T(2,128)(2,1)} %all-gather.5.cloned.1.call-done) | copy-start | bytes 7077892
  419.9 0.9 copy-start.4
Sparse Core Ops, SparseCore 0:
  58.0 113.2 all-reduce.2
  176.5 86.9 reduce-scatter.3
  267.6 58.5 all-gather.2
  329.6 60.4 all-gather.4
where the time goes:
time: 446 us; the launch traced here: 445 us
  waiting for transfers between devices  304 us (68%)
  starting transfers between devices  45 us (10%)
  local copies, waits for them, and re-layouts  32.7 us (7%)
  blocking collectives  25.6 us (6%)
  matrix products  18.7 us (4%)
  between operations  14.6 us (3%)
    unnamed x6, waiting for transfers between devices  166 us
    all_gather x1, waiting for transfers between devices, body(): lax.all_gather((active * up_pre).astype(jnp.bfloat16), 'dp', axis=2, tile...  59.7 us
    all_gather x1, waiting for transfers between devices, body(): segment = lax.all_gather(unit_share, 'dp', axis=3, tiled=True)  45.3 us
    all_to_all x2, starting transfers between devices, unpack_rows(): lax.all_to_all(shaped, 'expert', split_axis=1, concat_axis=1, tiled=True)  28.1 us
    all_to_all x1, blocking collectives, body(): lax.all_to_all(route_grad, 'expert', split_axis=1, concat_axis=1, tiled=T...  25.6 us
    all_to_all x1, waiting for transfers between devices, body(): lax.all_to_all(packed, 'expert', split_axis=1, concat_axis=1, tiled=True)  19.4 us
    all_to_all x1, starting transfers between devices, body(): lax.all_to_all(packed, 'expert', split_axis=1, concat_axis=1, tiled=True)  16.8 us
    all_to_all x2, waiting for transfers between devices, unpack_rows(): lax.all_to_all(shaped, 'expert', split_axis=1, concat_axis=1, tiled=True)  13.4 us
  transfers between devices with their start and end apart: 7, of which 6 were waited for; matrix products, arithmetic and copies ran while one was open for 9% of the time, Pallas kernels for 0%

commit v1 on v0

v1 whole, which is shorter than its diff:
```python
import functools

import jax
import jax.numpy as jnp
from jax import lax
from jax.experimental import pallas as pl
from jax.experimental.pallas import tpu as pltpu
from jax.sharding import PartitionSpec as P

ALL_EXP = 128
SIDE = 4
ROW = 16
MESH = pl.DeviceIdType.MESH
BF = jnp.bfloat16
F32 = jnp.float32


def dot(a, b, ca, cb):
    return lax.dot_general(a, b, (((ca,), (cb,)), ((), ())), preferred_element_type=F32)


def activation(values):
    sigma = jax.nn.sigmoid(values)
    return values * sigma, sigma * (1.0 + values * (1.0 - sigma))


class Ring:
    def __init__(self, place, device_of, send_sems, recv_sems):
        self.place, self.device_of = place, device_of
        self.send_sems, self.recv_sems = send_sems, recv_sems

    def at(self, step):
        return lax.rem(self.place + (step + SIDE), SIDE)

    def copy(self, number, src, dst, step):
        return pltpu.make_async_remote_copy(
            src_ref=src, dst_ref=dst, send_sem=self.send_sems.at[number], recv_sem=self.recv_sems.at[number],
            device_id=self.device_of(self.at(step)), device_id_type=MESH)


class ReduceScatter:
    def __init__(self, ring, block, tmp, summed, arrived, half):
        self.ring, self.block, self.tmp, self.summed = ring, block, tmp, summed
        r = ring
        self.first = (r.copy(0, block(r.at(2), 0), tmp.at[0], 1), r.copy(1, block(r.at(2), 1), tmp.at[1], -1))
        self.second = (r.copy(2, block(r.at(1), 1), half(arrived.at[0], 1), 1),
                       r.copy(3, block(r.at(-1), 0), half(arrived.at[1], 0), -1))
        self.third = (r.copy(4, summed.at[0], half(arrived.at[0], 0), 1),
                      r.copy(5, summed.at[1], half(arrived.at[1], 1), -1))

    def start(self):
        for c in self.first + self.second:
            c.start()

    def relay(self):
        for way, (step, h) in enumerate(((1, 0), (-1, 1))):
            self.first[way].wait_recv()
            mine = self.block(self.ring.at(step), h)[...]
            self.summed[way] = (mine.astype(F32) + self.tmp[way].astype(F32)).astype(BF)
            self.third[way].start()

    def wait(self):
        for c in self.second + self.third:
            c.wait_recv()

    def drain(self):
        for c in self.first + self.second + self.third:
            c.wait_send()


class AllGather:
    def __init__(self, ring, region):
        r = ring
        send = lambda number, q, h, step: r.copy(number, region(q, h), region(q, h), step)
        own, left, right = r.at(0), r.at(-1), r.at(1)
        self.first = (send(0, own, 0, 1), send(1, own, 1, -1))
        self.second = (send(2, own, 1, 1), send(3, own, 0, -1))
        self.third = (send(4, left, 0, 1), send(5, right, 1, -1))

    def start(self):
        for c in self.first + self.second:
            c.start()

    def relay(self):
        for way in range(2):
            self.first[way].wait_recv()
            self.third[way].start()

    def wait(self):
        for c in self.second + self.third:
            c.wait_recv()

    def drain(self):
        for c in self.first + self.second + self.third:
            c.wait_send()


def kernel(peers, cap, tok, ids, codes, ograd, win_hbm, wout_hbm, out, tgrad, wing_hbm, woutg_hbm,
           win, wout, wing, woutg, s_tok, s_gr, r_tok, r_gr, s_eo, s_ig, r_eo, r_ig, x, g, chosen_at, w_hi, w_lo, acc,
           pre, hg, hid, unit,
           t_g, m_g, a_g, s_g, t2_g, m2_g, a2_g,
           t_u, m_u, a_u, s_u, t2_u, m2_u, a2_u,
           t_h, m_h, a_h, s_h, t2_h, m2_h, a2_h,
           t_k, m_k, a_k, s_k, t2_k, m2_k, a2_k,
           send_sems, recv_sems, a2a_send, a2a_recv, local):
    dp, me = lax.axis_index("dp"), lax.axis_index("expert")
    px, py = dp // SIDE, lax.rem(dp, SIDE)
    rows, ff = x.shape[0], wout.shape[0]
    grp, quarter = rows // SIDE, ff // SIDE
    hgrp = grp // 2
    slots = peers * ROW

    barrier = pltpu.get_barrier_semaphore()

    @pl.loop(1, peers)
    def _(r):
        pl.semaphore_signal(barrier, inc=1, device_id=(dp, lax.rem(me + r, peers)), device_id_type=MESH)

    for step in (1, SIDE - 1):
        pl.semaphore_signal(barrier, inc=1, device_id=(lax.rem(px + step, SIDE) * SIDE + py, me), device_id_type=MESH)
        pl.semaphore_signal(barrier, inc=1, device_id=(px * SIDE + lax.rem(py + step, SIDE), me), device_id_type=MESH)

    load_in = pltpu.make_async_copy(win_hbm, win, local.at[0])
    load_out = pltpu.make_async_copy(wout_hbm, wout, local.at[1])
    load_in.start()
    load_out.start()

    count = tok.shape[0]
    at_slot = lax.broadcasted_iota(jnp.int32, (count, slots), 1)
    expert_of = lax.rem(at_slot // ROW + me, peers)
    code_values = codes[...].astype(F32)
    shares = code_values / jnp.sum(code_values, axis=1, keepdims=True)
    names = ids[...]
    chosen = jnp.zeros((count, slots), F32)
    weight = jnp.zeros((count, slots), F32)
    for k in range(names.shape[1]):
        hit = names[:, k:k + 1] == expert_of
        chosen = jnp.where(hit, 1.0, chosen)
        weight = jnp.where(hit, shares[:, k:k + 1], weight)
    earlier = (lax.broadcasted_iota(jnp.int32, (count, count), 0)
               > lax.broadcasted_iota(jnp.int32, (count, count), 1)).astype(F32).astype(BF)
    rank = dot(earlier, chosen.astype(BF), 1, 0)
    place = lax.rem(at_slot, ROW).astype(F32)
    here = (chosen > 0.5) & (rank == place)
    placed = jnp.where(here, 1.0, 0.0).astype(BF)
    weight = jnp.where(here, weight, 0.0)
    high = weight.astype(BF)
    chosen_at[...] = placed
    w_hi[...] = high
    w_lo[...] = (weight - high.astype(F32)).astype(BF)
    s_tok[...] = dot(placed, tok[...], 0, 0).astype(BF).reshape(s_tok.shape)

    pl.semaphore_wait(barrier, peers - 1 + 4)

    def exchange(number, send, recv, sign):
        def go(r):
            pltpu.make_async_remote_copy(
                src_ref=send.at[r], dst_ref=recv.at[r], send_sem=a2a_send.at[number], recv_sem=a2a_recv.at[number],
                device_id=(dp, lax.rem(me + sign * r + peers, peers)), device_id_type=MESH).start()

        @pl.loop(1, peers // 2)
        def _(r):
            go(r)
            go(peers - r)

        go(peers // 2)
        recv[0] = send[0]
        whole = send.at[pl.ds(1, peers - 1)], recv.at[pl.ds(1, peers - 1)]
        return pltpu.make_async_remote_copy(
            src_ref=whole[0], dst_ref=whole[1], send_sem=a2a_send.at[number], recv_sem=a2a_recv.at[number],
            device_id=(dp, lax.rem(me + 1, peers)), device_id_type=MESH)

    to_x = exchange(0, s_tok, r_tok, 1)
    both = dot(w_hi[...], ograd[...], 0, 0) + dot(w_lo[...], ograd[...], 0, 0)
    s_gr[...] = both.astype(BF).reshape(s_gr.shape)
    to_g = exchange(1, s_gr, r_gr, 1)

    slot_row = lax.broadcasted_iota(jnp.int32, (rows, slots), 1)
    slot_pos = lax.rem(slot_row, ROW)
    packed_row = jnp.where(slot_pos < cap, slot_row // ROW * cap + slot_pos, -1)
    squeeze = (packed_row == lax.broadcasted_iota(jnp.int32, (rows, slots), 0)).astype(F32).astype(BF)

    x_dev = lambda q: (q * SIDE + py, me)
    y_dev = lambda q: (px * SIDE + q, me)
    used = [0]

    def ring(along_x):
        first = used[0]
        used[0] += 6
        return Ring(px if along_x else py, x_dev if along_x else y_dev,
                    send_sems.at[pl.ds(first, 6)], recv_sems.at[pl.ds(first, 6)])

    span = lambda q: pl.ds(pl.multiple_of(q * quarter, 128), quarter)

    def scatter_pair(src, row0, height, col0, x_first, bufs, split):
        tmp, mid, arr, s, tmp2, mid2, arr2 = bufs
        rows_at = pl.ds(row0, height)
        if x_first:
            half_width = 2 * quarter
            block = lambda q, h: src.at[q, rows_at, pl.ds(col0 + h * half_width, half_width)]
            whole = lambda q: src.at[q, rows_at, pl.ds(col0, 4 * quarter)]
            half = lambda ref, h: ref.at[:, pl.ds(h * half_width, half_width)]
            sub = lambda q: s.at[:, span(q)]
        else:
            cols = lambda q: pl.ds(pl.multiple_of(col0 + q * quarter, 128), quarter)
            block = lambda q, h: src.at[pl.ds(2 * h, 2), rows_at, cols(q)]
            whole = lambda q: src.at[:, rows_at, cols(q)]
            half = lambda ref, h: ref.at[pl.ds(2 * h, 2)]
            sub = lambda q: s.at[q]
        one = ReduceScatter(ring(x_first), block, tmp, mid, arr, half)
        cut = lambda h: pl.ds(0, split) if h == 0 else pl.ds(split, height - split)
        pick = lambda ref, h: ref.at[cut(h)]
        two = ReduceScatter2(ring(not x_first), lambda q, h: pick(sub(q), h), tmp2, mid2, arr2, pick)
        own = px if x_first else py
        other = py if x_first else px

        def join():
            one.wait()
            s[...] = (whole(own)[...].astype(F32) + arr[0].astype(F32) + arr[1].astype(F32)).astype(BF)

        def result():
            two.wait()
            return sub(other)[...].astype(F32) + arr2[0].astype(F32) + arr2[1].astype(F32)

        return one, join, two, result

    class ReduceScatter2(ReduceScatter):
        def __init__(self, ring_, block, tmp, summed, arrived, half):
            class Pair:
                def __init__(self, refs):
                    self.at = refs

                def __getitem__(self, i):
                    return self.at[i][...]

                def __setitem__(self, i, value):
                    self.at[i][...] = value

            super().__init__(ring_, block, Pair(tmp), Pair(summed), arrived, half)

    def gather_pair(dst, row0, height, col0, x_first_scatter, split):
        rows_at = pl.ds(row0, height)
        cut = lambda h: pl.ds(row0, split) if h == 0 else pl.ds(row0 + split, height - split)
        cols = lambda q: pl.ds(pl.multiple_of(col0 + q * quarter, 128), quarter)
        if x_first_scatter:
            one = AllGather(ring(False), lambda q, h: dst.at[px, cut(h), cols(q)])
            two = AllGather(ring(True), lambda q, h: dst.at[q, rows_at, pl.ds(col0 + 2 * h * quarter, 2 * quarter)])
        else:
            one = AllGather(ring(True), lambda q, h: dst.at[q, cut(h), cols(py)])
            two = AllGather(ring(False), lambda q, h: dst.at[pl.ds(2 * h, 2), rows_at, cols(q)])
        return one, two

    gate1, gate_join, gate2, gate_sum = scatter_pair(
        pre, 0, grp, 0, True, (t_g, m_g, a_g, s_g, t2_g, m2_g, a2_g), grp // 2)
    up1, up_join, up2, up_sum = scatter_pair(
        pre, 0, grp, ff, False, (t_u, m_u, a_u, s_u, t2_u, m2_u, a2_u), grp // 2)
    hga1, hga_join, hga2, hga_sum = scatter_pair(
        hg, 0, hgrp, 0, True, (t_h, m_h, a_h, s_h, t2_h, m2_h, a2_h), 32)
    hgb1, hgb_join, hgb2, hgb_sum = scatter_pair(
        hg, hgrp, hgrp, 0, False, (t_k, m_k, a_k, s_k, t2_k, m2_k, a2_k), 32)
    hida1, hida2 = gather_pair(hid, 0, hgrp, 0, True, 32)
    hidb1, hidb2 = gather_pair(hid, hgrp, hgrp, 0, False, 32)
    ug1, ug2 = gather_pair(unit, 0, grp, 0, True, grp // 2)
    uu1, uu2 = gather_pair(unit, 0, grp, ff, False, grp // 2)

    load_in.wait()
    to_x.wait_recv()
    x[...] = dot(squeeze, r_tok[...].reshape(slots, -1), 1, 0).astype(BF)

    @pl.loop(0, 2 * SIDE)
    def _(n):
        cols = span(n)
        pre[:, :, cols] = dot(x[...], win[:, cols], 1, 0).astype(BF).reshape(SIDE, grp, quarter)

    gate1.start()
    up1.start()
    gate1.relay()
    up1.relay()

    load_out.wait()
    to_g.wait_recv()
    g[...] = dot(squeeze, r_gr[...].reshape(slots, -1), 1, 0).astype(BF)

    @pl.loop(0, SIDE)
    def _(n):
        cols = span(n)
        hg[:, :, cols] = dot(g[...], wout[cols, :], 1, 1).astype(BF).reshape(SIDE, grp, quarter)

    gate_join()
    gate2.start()
    up_join()
    up2.start()
    hga1.start()
    hgb1.start()
    gate2.relay()
    up2.relay()
    hga1.relay()
    hgb1.relay()

    gate_pre, up_pre = gate_sum(), up_sum()
    active, slopes = activation(gate_pre)
    hidden = (active * up_pre).astype(BF)
    hid[px, :, span(py)] = hidden
    hida1.start()
    hidb1.start()

    hga_join()
    hga2.start()
    hgb_join()
    hgb2.start()
    hida1.relay()
    hidb1.relay()
    hga2.relay()
    hgb2.relay()
    hida1.wait()
    hida2.start()
    hidb1.wait()
    hidb2.start()

    hidden_grad = jnp.concatenate([hga_sum(), hgb_sum()], axis=0)
    unit[px, :, span(py)] = (hidden_grad * up_pre * slopes).astype(BF)
    unit[px, :, pl.ds(pl.multiple_of(ff + py * quarter, 128), quarter)] = (hidden_grad * active).astype(BF)
    ug1.start()
    uu1.start()
    hida2.relay()
    hidb2.relay()
    ug1.relay()
    uu1.relay()
    ug1.wait()
    ug2.start()
    uu1.wait()
    uu2.start()

    row_slot = lax.broadcasted_iota(jnp.int32, (slots, rows), 0)
    row_pos = lax.rem(row_slot, ROW)
    from_row = jnp.where(row_pos < cap, row_slot // ROW * cap + row_pos, -1)
    spread = (from_row == lax.broadcasted_iota(jnp.int32, (slots, rows), 1)).astype(F32).astype(BF)

    hida2.wait()
    hidb2.wait()
    acc[...] = jnp.zeros_like(acc)

    @pl.loop(0, SIDE)
    def _(n):
        cols = span(n)
        acc[...] += dot(hid[:, :, cols].reshape(rows, quarter), wout[cols, :], 1, 0)

    s_eo[...] = dot(spread, acc[...].astype(BF), 1, 0).astype(BF).reshape(s_eo.shape)
    from_eo = exchange(2, s_eo, r_eo, -1)

    ug2.relay()
    uu2.relay()

    @pl.loop(0, SIDE)
    def _(n):
        cols = span(n)
        woutg[cols, :] = dot(hid[:, :, cols].reshape(rows, quarter), g[...], 0, 0).astype(BF)

    store_out = pltpu.make_async_copy(woutg, woutg_hbm, local.at[2])
    store_out.start()

    ug2.wait()
    uu2.wait()
    acc[...] = jnp.zeros_like(acc)

    @pl.loop(0, 2 * SIDE)
    def _(n):
        cols = span(n)
        acc[...] += dot(unit[:, :, cols].reshape(rows, quarter), win[:, cols], 1, 1)

    s_ig[...] = dot(spread, acc[...].astype(BF), 1, 0).astype(BF).reshape(s_ig.shape)
    from_ig = exchange(3, s_ig, r_ig, -1)

    @pl.loop(0, 2 * SIDE)
    def _(n):
        cols = span(n)
        wing[:, cols] = dot(x[...], unit[:, :, cols].reshape(rows, quarter), 0, 0).astype(BF)

    store_in = pltpu.make_async_copy(wing, wing_hbm, local.at[3])
    store_in.start()

    from_eo.wait_recv()
    returned = r_eo[...].reshape(slots, -1)
    out[...] = (dot(w_hi[...], returned, 1, 0) + dot(w_lo[...], returned, 1, 0)).astype(BF)
    from_ig.wait_recv()
    tgrad[...] = dot(chosen_at[...], r_ig[...].reshape(slots, -1), 1, 0).astype(BF)

    for stage in (gate1, gate2, up1, up2, hga1, hga2, hgb1, hgb2, hida1, hida2, hidb1, hidb2, ug1, ug2, uu1, uu2):
        stage.drain()
    for moved in (to_x, to_g, from_eo, from_ig):
        moved.wait_send()
    store_out.wait()
    store_in.wait()


def body(tokens, expert_ids, gate_codes, out_grad, w_in, w_out):
    peers = lax.axis_size("expert")
    count, width = tokens.shape
    top = expert_ids.shape[1]
    ff = w_out.shape[1]
    cap = 3 * count * top // (2 * ALL_EXP)
    rows = cap * peers
    grp, quarter = rows // SIDE, ff // SIDE
    slots = peers * ROW
    vm = lambda *shape: pltpu.VMEM(shape, BF)

    def sums(height, x_first, split):
        if x_first:
            halves, block = (height, 2 * quarter), (height, 4 * quarter)
        else:
            halves, block = (2, height, quarter), (4, height, quarter)
        pair = [vm(split, quarter), vm(height - split, quarter)]
        return [vm(2, *halves), vm(2, *halves), vm(2, *block), vm(*block), pair, list(pair), vm(2, height, quarter)]

    message = vm(peers, ROW, width)
    scratch = [
        vm(width, 2 * ff), vm(ff, width), vm(width, 2 * ff), vm(ff, width),
        message, message, message, message, message, message, message, message,
        vm(rows, width), vm(rows, width), vm(count, slots), vm(count, slots), vm(count, slots),
        pltpu.VMEM((rows, width), F32),
        vm(SIDE, grp, 2 * ff), vm(SIDE, grp, ff), vm(SIDE, grp, ff), vm(SIDE, grp, 2 * ff),
        *sums(grp, True, grp // 2), *sums(grp, False, grp // 2),
        *sums(grp // 2, True, 32), *sums(grp // 2, False, 32),
        pltpu.SemaphoreType.DMA((96,)), pltpu.SemaphoreType.DMA((96,)),
        pltpu.SemaphoreType.DMA((4,)), pltpu.SemaphoreType.DMA((4,)), pltpu.SemaphoreType.DMA((4,)),
    ]
    vmem, hbm = pl.BlockSpec(memory_space=pltpu.VMEM), pl.BlockSpec(memory_space=pl.ANY)
    out, tgrad, wing, woutg = pl.pallas_call(
        functools.partial(kernel, peers, cap),
        out_shape=(
            jax.ShapeDtypeStruct((count, width), BF), jax.ShapeDtypeStruct((count, width), BF),
            jax.ShapeDtypeStruct((width, 2 * ff), BF), jax.ShapeDtypeStruct((ff, width), BF)),
        in_specs=[vmem, vmem, vmem, vmem, hbm, hbm],
        out_specs=(vmem, vmem, hbm, hbm),
        scratch_shapes=scratch,
        compiler_params=pltpu.CompilerParams(
            collective_id=0, has_side_effects=True, vmem_limit_bytes=56 * 1024 * 1024),
        cost_estimate=pl.CostEstimate(
            flops=2 * rows * width * ff * 9, bytes_accessed=12 * width * ff, transcendentals=grp * quarter),
    )(tokens, expert_ids, gate_codes, out_grad, w_in[0], w_out[0])
    return out, tgrad, wing[None], woutg[None]


def solution(mesh):
    placed = (
        P("expert", "dp"),
        P("expert", None),
        P("expert", None),
        P("expert", "dp"),
        P("expert", "dp", None),
        P("expert", None, "dp"),
    )
    return jax.shard_map(
        body,
        mesh=mesh,
        in_specs=placed,
        out_specs=(
            P("expert", "dp"),
            P("expert", "dp"),
            P("expert", "dp", None),
            P("expert", None, "dp"),
        ),
        check_vma=False,
    )
```

time: 446 us -> 112 us (0.25)
  waiting for transfers between devices: 304 us -> 0 us
  Pallas kernels: 0 us -> 102 us
  starting transfers between devices: 45 us -> 0 us
  blocking collectives: 25.6 us -> 0 us
  local copies, waits for them, and re-layouts: 32.7 us -> 9.38 us
  matrix products: 18.7 us -> 0 us
  between operations: 14.6 us -> 0.64 us
    unnamed x6 -> x0, waiting for transfers between devices: 166 us -> none
    all_gather x2 -> x0, waiting for transfers between devices: 105 us -> none  [the longest x1 59.7 us: body(): lax.all_gather((active * up_pre).astype(jnp.bfloat16), 'dp', axis=2, tile...]
    pallas_call x0 -> x1, Pallas kernels: none -> 102 us  [body(): pl.pallas_call(functools.partial(kernel, peers, cap), out_shape=(jax.Shap...]
    all_to_all x3 -> x0, starting transfers between devices: 44.8 us -> none  [the longest x2 28.1 us: unpack_rows(): lax.all_to_all(shaped, 'expert', split_axis=1, concat_axis=1, tiled=True)]
    all_to_all x3 -> x0, waiting for transfers between devices: 32.8 us -> none  [the longest x1 19.4 us: body(): lax.all_to_all(packed, 'expert', split_axis=1, concat_axis=1, tiled=True)]
    all_to_all x1 -> x0, blocking collectives: 25.6 us -> none  [body(): lax.all_to_all(route_grad, 'expert', split_axis=1, concat_axis=1, tiled=T...]
    dot_general x11 -> x0, matrix products: 18.7 us -> none  [the longest x1 2.88 us: body(): jnp.einsum('lrgf,ldgf->lrd', segment, w_in_split, preferred_element_type=...]
    all_gather x1 -> x0, local copies, waits for them, and re-layouts: 5.64 us -> none  [body(): segment = lax.all_gather(unit_share, 'dp', axis=3, tiled=True)]
  transfers between devices with their start and end apart: 7 -> 0, of which waited for: 6 -> 0; matrix products, arithmetic and copies ran while one was open for 9% -> 0% of each run, Pallas kernels for 0% -> 0%
where the time goes in v1:
time: 112 us
  Pallas kernels  102 us (91%)
  local copies, waits for them, and re-layouts  9.38 us (8%)
    pallas_call x1, Pallas kernels, body(): pl.pallas_call(functools.partial(kernel, peers, cap), out_shape=(jax.Shap...  102 us
    unnamed x8, local copies, waits for them, and re-layouts  9.38 us

profile of v1, /device:TPU:1, one launch (start us, length us, event | category | flops | bytes accessed | tf_op | source)
XLA Modules:
  0.0 112.1 jit_solution(17373999714459257423)
XLA Ops:
  0.6 1.4 %copy.10.ids = s32[128,8]{1,0:T(8,128)} copy(s32[128,8]{0,1:T(8,128)} %param.7) | data formatting | bytes 8192 | tf_op args[1]
  2.0 1.4 %copy.11.codes = s32[128,8]{1,0:T(8,128)} copy(s32[128,8]{0,1:T(8,128)} %param.8) | data formatting | bytes 8192 | tf_op args[2]
  3.5 102.0 %shard_map.93 = (bf16[128,256]{1,0:T(8,128)(2,1)}, bf16[128,256]{1,0:T(8,128)(2,1)}, bf16[256,3072]{1,0:T(8,128)(2,1)}, bf16[1536,256]{1,0:T(8,128)(2,1)}) custom-call(bf16[128,256]{1,0:T(8,128)(2,1)} %tok.1, s32[128,8]{1,0:T(8,128)} %copy.10.ids, s32[128,8]{1,0:T(8,128)} %copy.11.codes, bf16[128,256]{1,0:T(8,128)(2,1)} %ograd.1, bf16[256,3072]{1,0:T(8,128)(2,1)} %bitcast.6, ...), custom_call_target="tpu_custom_call" | custom-call | flops 2717908992 | bytes 4718592 | tf_op jit(solution)/shard_map/pallas_call | solution.py:428
  105.5 1.5 %copy.16 = bf16[128,256]{1,0:T(8,128)(2,1)} copy(bf16[128,256]{1,0:T(8,128)(2,1)} %get-tuple-element.16) | data formatting | bytes 131072
  107.0 1.5 %copy.17 = bf16[128,256]{1,0:T(8,128)(2,1)} copy(bf16[128,256]{1,0:T(8,128)(2,1)} %get-tuple-element.17) | data formatting | bytes 131072
  108.4 0.0 copy-start
  108.4 2.7 %copy.18 = bf16[1,256,3072]{2,1,0:T(8,128)(2,1)} copy(bf16[1,256,3072]{2,1,0:T(8,128)(2,1)} %bitcast.4) | data formatting | bytes 3145728
  111.2 0.0 copy-done
  111.2 0.9 copy.19
Async XLA Ops:
  108.4 2.7 %copy-start = (bf16[1536,256]{1,0:T(8,128)(2,1)S(1)}, bf16[1536,256]{1,0:T(8,128)(2,1)}, u32[]{:S(2)}) copy-start(bf16[1536,256]{1,0:T(8,128)(2,1)} %get-tuple-element.11) | copy-start | bytes 2359300

commit v2 on v0

v2 whole, which is shorter than its diff:
```python
import functools

import jax
import jax.numpy as jnp
from jax import lax
from jax.experimental import pallas as pl
from jax.experimental.pallas import tpu as pltpu
from jax.sharding import PartitionSpec as P

ALL_EXP = 128
SIDE = 4
LANES = 128
MESH = pl.DeviceIdType.MESH
BF = jnp.bfloat16
F32 = jnp.float32


def dot(a, b, ca, cb):
    return lax.dot_general(a, b, (((ca,), (cb,)), ((), ())), preferred_element_type=F32)


def activation(values):
    sigma = jax.nn.sigmoid(values)
    return values * sigma, sigma * (1.0 + values * (1.0 - sigma))


def iota(shape, axis):
    return lax.broadcasted_iota(jnp.int32, shape, axis)


def mask(condition):
    return jnp.where(condition, 1.0, 0.0).astype(BF)


class Move:
    def __init__(self, started, **kw):
        self.started, self.move = started, pltpu.make_async_remote_copy(device_id_type=MESH, **kw)
        self.arrived = self.left = False

    def start(self):
        self.move.start()
        self.started.append(self)

    def wait(self):
        self.arrived = True
        self.move.wait_recv()

    def leave(self):
        if not self.left:
            self.left = True
            self.move.wait_send()


class Ring:
    def __init__(self, started, place, device_of, send_sems, recv_sems):
        self.started, self.place, self.device_of = started, place, device_of
        self.send_sems, self.recv_sems = send_sems, recv_sems

    def at(self, step):
        return lax.rem(self.place + (step + SIDE), SIDE)

    def copy(self, number, src, dst, step):
        return Move(self.started, src_ref=src, dst_ref=dst, send_sem=self.send_sems.at[number],
                    recv_sem=self.recv_sems.at[number], device_id=self.device_of(self.at(step)))


class Stage:
    def start(self):
        for c in self.first + self.second:
            c.start()

    def wait(self):
        for c in self.second + self.third:
            c.wait()


class ReduceScatter(Stage):
    def __init__(self, ring, block, tmp, summed, arrived):
        self.ring, self.block, self.tmp, self.summed = ring, block, tmp, summed
        r = ring
        self.first = (r.copy(0, block(r.at(2), 0), tmp[0], 1), r.copy(1, block(r.at(2), 1), tmp[1], -1))
        self.second = (r.copy(2, block(r.at(1), 1), arrived(0, 1), 1), r.copy(3, block(r.at(-1), 0), arrived(1, 0), -1))
        self.third = (r.copy(4, summed[0], arrived(0, 0), 1), r.copy(5, summed[1], arrived(1, 1), -1))

    def relay(self):
        for way, (step, h) in enumerate(((1, 0), (-1, 1))):
            self.first[way].wait()
            mine = self.block(self.ring.at(step), h)[...]
            self.summed[way][...] = (mine.astype(F32) + self.tmp[way][...].astype(F32)).astype(BF)
            self.third[way].start()


class AllGather(Stage):
    def __init__(self, ring, region):
        r = ring
        send = lambda number, q, h, step: r.copy(number, region(q, h), region(q, h), step)
        own, left, right = r.at(0), r.at(-1), r.at(1)
        self.first = (send(0, own, 0, 1), send(1, own, 1, -1))
        self.second = (send(2, own, 1, 1), send(3, own, 0, -1))
        self.third = (send(4, left, 0, 1), send(5, right, 1, -1))

    def relay(self):
        for way in range(2):
            self.first[way].wait()
            self.third[way].start()


class Direct(Stage):
    def __init__(self, ring, out, into):
        self.moves = [ring.copy(way, out(ring.at(step)), into(way, ring.at(step)), step)
                      for way, step in enumerate((2, 1, -1))]

    def start(self):
        for c in self.moves:
            c.start()

    def wait(self):
        for c in self.moves:
            c.wait()


def span(q, width, first=0):
    return pl.ds(pl.multiple_of(q * width + first, LANES), width)


class Half:
    def __init__(self, x_first, height, width, src, dst, bufs, spots, ring):
        px, py = spots
        self.x_first, self.src, self.dst, self.width, self.spots = x_first, src, dst, width, spots
        tmp, mid, arr, s, arr2 = bufs
        self.arr, self.s, self.arr2 = arr, s, arr2
        wide = lambda h: pl.ds(h * 2 * width, 2 * width)
        pair = lambda h: pl.ds(2 * h, 2)
        if x_first:
            block = lambda q, h: src.at[q, :, wide(h)]
            self.whole = lambda: src.at[px]
            arrived = lambda way, h: arr.at[way, :, wide(h)]
            self.sub = lambda q: s.at[:, span(q, width)]
            own = dst.at[px, :, span(py, width)]
            region2 = lambda q, h: dst.at[q, :, wide(h)]
        else:
            block = lambda q, h: src.at[pair(h), :, span(q, width)]
            self.whole = lambda: src.at[:, :, span(py, width)]
            arrived = lambda way, h: arr.at[way, pair(h)]
            self.sub = lambda q: s.at[q]
            own = dst.at[px, :, span(py, width)]
            region2 = lambda q, h: dst.at[pair(h), :, span(q, width)]
        self.sum1 = ReduceScatter(ring(x_first), block, (tmp.at[0], tmp.at[1]), (mid.at[0], mid.at[1]), arrived)
        self.sum2 = Direct(ring(not x_first), self.sub, lambda way, q: arr2.at[way])
        self.get1 = Direct(ring(not x_first), lambda q: own, lambda way, q: own)
        self.get2 = AllGather(ring(x_first), region2)

    @staticmethod
    def scratch(x_first, height, width):
        vm = lambda *shape: pltpu.VMEM(shape, BF)
        half, block = ((height, 2 * width), (height, 4 * width)) if x_first else ((2, height, width), (4, height, width))
        return [vm(2, *half), vm(2, *half), vm(2, *block), vm(*block), vm(3, height, width)]

    def join(self):
        self.sum1.wait()
        self.s[...] = (self.whole()[...].astype(F32) + self.arr[0].astype(F32) + self.arr[1].astype(F32)).astype(BF)
        self.sum2.start()

    def result(self):
        self.sum2.wait()
        other = self.spots[1] if self.x_first else self.spots[0]
        return self.sub(other)[...].astype(F32) + sum(self.arr2[way].astype(F32) for way in range(3))

    def put(self, value):
        px, py = self.spots
        self.dst[px, :, span(py, self.width)] = value.astype(BF)
        self.get1.start()

    def onward(self):
        self.get1.wait()
        self.get2.start()


def both(halves, step, stage=None):
    for half in halves:
        getattr(getattr(half, stage) if stage else half, step)()


def steps(peers, cap, tok, ids, codes, ograd, win_hbm, wout_hbm, out, tgrad, wing_hbm, woutg_hbm,
          win, wout, wing, woutg, s1, s2, r1, r2, b1, b2, e1, e2, xs, gs, back1, back2,
          sq, sp, sq2, sp2, partial, gathered, bufs, send_sems, recv_sems, z_send, z_recv, local, started):
    dp, me = lax.axis_index("dp"), lax.axis_index("expert")
    px, py = dp // SIDE, lax.rem(dp, SIDE)
    ff, count = wout.shape[0], tok.shape[0]
    quarter = ff // SIDE
    height = partial[0].shape[1]
    rows = SIDE * height
    near = peers // 2
    edge = near // 2
    one, two = s1.shape[1], s2.shape[1]

    barrier = pltpu.get_barrier_semaphore()

    @pl.loop(1, peers)
    def _(r):
        pl.semaphore_signal(barrier, inc=1, device_id=(dp, lax.rem(me + r, peers)), device_id_type=MESH)

    for step in range(1, SIDE):
        pl.semaphore_signal(barrier, inc=1, device_id=(lax.rem(px + step, SIDE) * SIDE + py, me), device_id_type=MESH)
        pl.semaphore_signal(barrier, inc=1, device_id=(px * SIDE + lax.rem(py + step, SIDE), me), device_id_type=MESH)

    load_in = pltpu.make_async_copy(win_hbm, win, local.at[0])
    load_out = pltpu.make_async_copy(wout_hbm, wout, local.at[1])
    load_in.start()
    load_out.start()

    slot = iota((peers, count), 0)
    away = jnp.where(slot > edge, slot - edge, jnp.where(slot > 0, slot - edge - 1 + peers, 0))
    expert_of = lax.rem(away + me, peers)
    names = ids[...]
    code_values = codes[...].astype(F32)
    shares = code_values / jnp.sum(code_values, axis=0, keepdims=True)
    chosen = jnp.zeros((peers, count), F32)
    weight = jnp.zeros((peers, count), F32)
    for k in range(names.shape[0]):
        hit = names[k:k + 1, :] == expert_of
        chosen = jnp.where(hit, 1.0, chosen)
        weight = jnp.where(hit, shares[k:k + 1, :], weight)
    earlier = mask(iota((count, count), 0) < iota((count, count), 1))
    rank = dot(chosen.astype(BF), earlier, 1, 0)
    rank = jnp.where(chosen > 0.5, rank, 200.0).astype(BF)
    high = weight.astype(BF)
    low = (weight - high.astype(F32)).astype(BF)

    def places(size):
        widen = mask(iota((peers * size, peers), 0) // size == iota((peers * size, peers), 1))
        spot = lax.rem(iota((peers * size, count), 0), size)
        return spot, dot(widen, rank, 1, 0), dot(widen, high, 1, 0), dot(widen, low, 1, 0)

    keep = lambda here, value: jnp.where(here, value, 0.0).astype(BF)
    spot, at, hi, lo = places(one)
    left = (spot < cap) & (at == spot.astype(F32))
    right = (spot >= cap) & (spot < 2 * cap) & (at == (spot - cap).astype(F32))
    rest = (spot >= 2 * cap) & (at == (spot - 3 * cap + two).astype(F32))
    tokens, grads = tok[...], ograd[...]
    table = jnp.concatenate([mask(left), mask(right), keep(rest, hi), keep(rest, lo)], axis=1)
    values = jnp.concatenate([tokens[:, :LANES], tokens[:, LANES:], grads[:, LANES:], grads[:, LANES:]], axis=0)
    s1[...] = dot(table, values, 1, 0).astype(BF).reshape(s1.shape)
    back1[...] = table
    spot, at, hi, lo = places(two)
    left = (spot < cap) & (at == spot.astype(F32))
    right = (spot >= cap) & (at == (spot - cap).astype(F32))
    table = jnp.concatenate([keep(left, hi), keep(left, lo), keep(right, hi), keep(right, lo)], axis=1)
    values = jnp.concatenate([grads[:, :LANES], grads[:, :LANES], grads[:, LANES:], grads[:, LANES:]], axis=0)
    s2[...] = dot(table, values, 1, 0).astype(BF).reshape(s2.shape)
    back2[...] = table

    pl.semaphore_wait(barrier, peers - 1 + 2 * (SIDE - 1))

    def exchange(number, send, recv, chunk, sign):
        def go(k):
            away = jnp.where(k > edge, k - edge, k - edge - 1 + peers)
            pltpu.make_async_remote_copy(
                src_ref=send.at[k], dst_ref=recv.at[k], send_sem=z_send.at[number], recv_sem=z_recv.at[number],
                device_id=(dp, lax.rem(me + sign * away + peers, peers)), device_id_type=MESH).start()

        if chunk == 0:
            @pl.loop(0, edge - 1)
            def _(i):
                go(edge - i)
                go(edge + 1 + i)

            go(1)
            recv[0] = send[0]
        else:
            @pl.loop(0, near // 2)
            def _(i):
                go(near + i)
                go(peers - 1 - i)

        span_of = pl.ds(1, near - 1) if chunk == 0 else pl.ds(near, near)
        move = Move(started, src_ref=send.at[span_of], dst_ref=recv.at[span_of], send_sem=z_send.at[number],
                    recv_sem=z_recv.at[number], device_id=(dp, lax.rem(me + 1, peers)))
        started.append(move)
        return move

    x0 = exchange(0, s1, r1, 0, 1)
    g0 = exchange(1, s2, r2, 0, 1)
    x0.leave()
    g0.leave()
    x1 = exchange(2, s1, r1, 1, 1)
    g1 = exchange(3, s2, r2, 1, 1)
    def matches(size, shape, axis, first, last, shift):
        at, row = iota(shape, axis), iota(shape, 1 - axis)
        spot = lax.rem(at, size)
        return mask((spot >= first) & (spot < last) & (row == at // size * cap + spot - shift))

    for i, part in enumerate(((0, cap, 0), (cap, 2 * cap, cap), (2 * cap, one, 3 * cap - two))):
        sq[i] = matches(one, (rows, near * one), 1, *part)
        sp[i] = matches(one, (near * one, rows), 0, *part)
    for i, part in enumerate(((0, cap, 0), (cap, two, cap))):
        sq2[i] = matches(two, (rows, near * two), 1, *part)
        sp2[i] = matches(two, (near * two, rows), 0, *part)

    used = [0]

    def ring(along_x):
        first = used[0]
        used[0] += 6
        device_of = (lambda q: (q * SIDE + py, me)) if along_x else (lambda q: (px * SIDE + q, me))
        return Ring(started, px if along_x else py, device_of, send_sems.at[pl.ds(first, 6)], recv_sems.at[pl.ds(first, 6)])

    halves = [Half(i % 2 == 0, height, partial[i].shape[2] // SIDE, partial[i], gathered[i], bufs[i], (px, py), ring)
              for i in range(6)]
    a, pre, hg = halves[0:2], halves[2:4], halves[4:6]

    def take_x(chunk):
        got = r1[pl.ds(chunk * near, near)].reshape(near * one, LANES)
        xs[chunk] = jnp.concatenate([dot(sq[0], got, 1, 0), dot(sq[1], got, 1, 0)], axis=1).astype(BF)

    def take_g(chunk):
        got = r1[pl.ds(chunk * near, near)].reshape(near * one, LANES)
        got2 = r2[pl.ds(chunk * near, near)].reshape(near * two, LANES)
        gs[chunk] = jnp.concatenate(
            [dot(sq2[0], got2, 1, 0), dot(sq2[1], got2, 1, 0) + dot(sq[2], got, 1, 0)], axis=1).astype(BF)

    def products(chunk, ref, first, width, left, q):
        ref[:, :, pl.ds(pl.multiple_of(q * (ref.shape[2] // SIDE) + first, LANES), width)] = (
            left.astype(BF).reshape(SIDE, height, width))

    cut0, cut1 = 256, 128

    load_in.wait()
    load_out.wait()
    x0.wait()
    g0.wait()
    take_x(0)
    take_g(0)

    @pl.loop(0, SIDE)
    def _(q):
        products(0, partial[0], 0, quarter, dot(xs[0], win[:, span(q, quarter)], 1, 0), q)
        products(0, partial[1], 0, quarter, dot(xs[0], win[:, span(q, quarter, ff)], 1, 0), q)
        grad = dot(gs[0], wout[span(q, quarter), :], 1, 1)
        products(0, partial[0], quarter, cut0, grad[:, :cut0], q)
        products(0, partial[1], quarter, quarter - cut0, grad[:, cut0:], q)

    both(a, "start", "sum1")
    both(a, "relay", "sum1")
    both(a, "join")

    x1.wait()
    take_x(1)

    @pl.loop(0, SIDE)
    def _(q):
        products(1, partial[2], 0, quarter, dot(xs[1], win[:, span(q, quarter)], 1, 0), q)
        products(1, partial[3], 0, quarter, dot(xs[1], win[:, span(q, quarter, ff)], 1, 0), q)

    both(pre, "start", "sum1")

    first, second = a[0].result(), a[1].result()
    gate_pre, up_pre = first[:, :quarter], second[:, :quarter]
    hidden_grad = jnp.concatenate([first[:, quarter:], second[:, quarter:]], axis=1)
    active, slopes = activation(gate_pre)
    hidden = active * up_pre
    a[0].put(jnp.concatenate([hidden_grad * up_pre * slopes, hidden[:, :cut0]], axis=1))
    a[1].put(jnp.concatenate([hidden_grad * active, hidden[:, cut0:]], axis=1))

    both(pre, "relay", "sum1")

    g1.wait()
    take_g(1)

    @pl.loop(0, SIDE)
    def _(q):
        grad = dot(gs[1], wout[span(q, quarter), :], 1, 1)
        products(1, partial[4], 0, cut1, grad[:, :cut1], q)
        products(1, partial[5], 0, quarter - cut1, grad[:, cut1:], q)

    both(hg, "start", "sum1")
    both(pre, "join")
    both(hg, "relay", "sum1")
    both(a, "onward")
    both(hg, "join")

    gate_pre, up_pre = pre[0].result(), pre[1].result()
    active, slopes = activation(gate_pre)
    hidden = active * up_pre
    hg[0].put(hidden[:, :cut1])
    hg[1].put(hidden[:, cut1:])
    hidden_grad = jnp.concatenate([hg[0].result(), hg[1].result()], axis=1)
    pre[0].put(hidden_grad * up_pre * slopes)
    pre[1].put(hidden_grad * active)
    both(a, "relay", "get2")
    both(hg, "onward")
    both(pre, "onward")
    both(hg, "relay", "get2")

    flat = lambda ref, where: ref[:, :, where].reshape(rows, -1)
    at = lambda q, chunk, first, width: pl.ds(pl.multiple_of(q * (gathered[chunk].shape[2] // SIDE) + first, LANES), width)

    def hidden_of(chunk, q):
        i, first, cut = (0, quarter, cut0) if chunk == 0 else (4, 0, cut1)
        return (flat(gathered[i], at(q, i, first, cut)), flat(gathered[i + 1], at(q, i + 1, first, quarter - cut)), cut)

    def unit_of(chunk, part, q):
        i = part if chunk == 0 else 2 + part
        return flat(gathered[i], at(q, i, 0, quarter))

    def outs(chunk):
        total = jnp.zeros((rows, 2 * LANES), F32)
        for q in range(SIDE):
            left, right, cut = hidden_of(chunk, q)
            total += dot(left, wout[pl.ds(q * quarter, cut), :], 1, 0)
            total += dot(right, wout[pl.ds(q * quarter + cut, quarter - cut), :], 1, 0)
        return total.astype(BF)

    def inputs(chunk):
        total = jnp.zeros((rows, 2 * LANES), F32)
        for part in range(2):
            for q in range(SIDE):
                total += dot(unit_of(chunk, part, q), win[:, pl.ds(part * ff + q * quarter, quarter)], 1, 1)
        return total.astype(BF)

    def return_outs(chunk, outs_):
        left, right = outs_[:, :LANES], outs_[:, LANES:]
        b2[pl.ds(chunk * near, near)] = (dot(sp2[0], left, 1, 0) + dot(sp2[1], right, 1, 0)).astype(BF).reshape(near, two, LANES)
        return exchange(4 + chunk, b2, e2, chunk, -1)

    def return_inputs(chunk, outs_, inputs_):
        left, right = inputs_[:, :LANES], inputs_[:, LANES:]
        b1[pl.ds(chunk * near, near)] = (
            dot(sp[0], left, 1, 0) + dot(sp[1], right, 1, 0) + dot(sp[2], outs_[:, LANES:], 1, 0)
        ).astype(BF).reshape(near, one, LANES)
        return exchange(6 + chunk, b1, e1, chunk, -1)

    both(a, "wait", "get2")
    near_outs = outs(0)
    eo0 = return_outs(0, near_outs)
    ig0 = return_inputs(0, near_outs, inputs(0))
    both(pre, "relay", "get2")
    both(hg, "wait", "get2")
    far_outs = outs(1)
    eo1 = return_outs(1, far_outs)

    @pl.loop(0, SIDE)
    def _(q):
        left0, right0, _ = hidden_of(0, q)
        left1, right1, _ = hidden_of(1, q)
        hidden0 = jnp.concatenate([left0, right0], axis=1)
        hidden1 = jnp.concatenate([left1, right1], axis=1)
        woutg[span(q, quarter), :] = (dot(hidden0, gs[0], 0, 0) + dot(hidden1, gs[1], 0, 0)).astype(BF)

    store_out = pltpu.make_async_copy(woutg, woutg_hbm, local.at[2])
    store_out.start()

    both(pre, "wait", "get2")
    ig1 = return_inputs(1, far_outs, inputs(1))

    for part in range(2):
        @pl.loop(0, SIDE)
        def _(q):
            wing[:, span(q, quarter, part * ff)] = (
                dot(xs[0], unit_of(0, part, q), 0, 0) + dot(xs[1], unit_of(1, part, q), 0, 0)).astype(BF)

    store_in = pltpu.make_async_copy(wing, wing_hbm, local.at[3])
    store_in.start()

    eo0.wait()
    eo1.wait()
    ret2 = e2[...].reshape(peers * two, LANES)
    sides = [dot(back2[:, pl.ds(i * LANES, LANES)], ret2, 0, 0) for i in range(4)]
    ig0.wait()
    ig1.wait()
    ret1 = e1[...].reshape(peers * one, LANES)
    ends = [dot(back1[:, pl.ds(i * LANES, LANES)], ret1, 0, 0) for i in range(4)]
    out[...] = jnp.concatenate([sides[0] + sides[1], sides[2] + sides[3] + ends[2] + ends[3]], axis=1).astype(BF)
    tgrad[...] = jnp.concatenate([ends[0], ends[1]], axis=1).astype(BF)
    store_out.wait()
    store_in.wait()


def kernel(peers, cap, *refs):
    started = []
    steps(peers, cap, *refs, started)
    for move in started:
        if not move.arrived:
            move.wait()
    for move in started:
        move.leave()


def finish(parts, *refs):
    srcs, dsts, holds, ins, outs = refs[:4], refs[4:8], refs[8:12], refs[12], refs[13]
    ways = []
    for src, dst, hold, cuts in zip(srcs, dsts, holds, parts):
        step = src.shape[0] // cuts
        for i in range(cuts):
            at, n = pl.ds(i * step, step), len(ways)
            ways.append((pltpu.make_async_copy(src.at[at], hold.at[at], ins.at[n]),
                         pltpu.make_async_copy(hold.at[at], dst.at[at], outs.at[n])))
    for load, _ in ways:
        load.start()
    for load, store in ways:
        load.wait()
        store.start()
    for _, store in ways:
        store.wait()


def body(tokens, expert_ids, gate_codes, out_grad, w_in, w_out):
    peers = lax.axis_size("expert")
    count, width = tokens.shape
    top = expert_ids.shape[1]
    ff = w_out.shape[1]
    cap = 3 * count * top // (2 * ALL_EXP)
    rows = cap * peers // 2
    height, quarter = rows // SIDE, ff // SIDE
    one, two = 32, 16
    vm = lambda *shape: pltpu.VMEM(shape, BF)
    widths = (quarter + 256, quarter + 128, quarter, quarter, 128, 256)
    m1, m2 = vm(peers, one, LANES), vm(peers, two, LANES)
    scratch = [
        vm(width, 2 * ff), vm(ff, width), vm(width, 2 * ff), vm(ff, width),
        m1, m2, m1, m2, m1, m2, m1, m2,
        vm(2, rows, width), vm(2, rows, width),
        vm(peers * one, 4 * count), vm(peers * two, 4 * count),
        vm(3, rows, peers // 2 * one), vm(3, peers // 2 * one, rows),
        vm(2, rows, peers // 2 * two), vm(2, peers // 2 * two, rows),
        [vm(SIDE, height, SIDE * w) for w in widths],
        [vm(SIDE, height, SIDE * w) for w in widths],
        [Half.scratch(i % 2 == 0, height, w) for i, w in enumerate(widths)],
        pltpu.SemaphoreType.DMA((144,)), pltpu.SemaphoreType.DMA((144,)),
        pltpu.SemaphoreType.DMA((8,)), pltpu.SemaphoreType.DMA((8,)), pltpu.SemaphoreType.DMA((4,)),
    ]
    vmem, hbm = pl.BlockSpec(memory_space=pltpu.VMEM), pl.BlockSpec(memory_space=pl.ANY)
    shapes = (
        jax.ShapeDtypeStruct((count, width), BF), jax.ShapeDtypeStruct((count, width), BF),
        jax.ShapeDtypeStruct((width, 2 * ff), BF), jax.ShapeDtypeStruct((ff, width), BF))
    results = pl.pallas_call(
        functools.partial(kernel, peers, cap),
        out_shape=shapes,
        in_specs=[vmem, vmem, vmem, vmem, hbm, hbm],
        out_specs=(vmem, vmem, hbm, hbm),
        scratch_shapes=scratch,
        compiler_params=pltpu.CompilerParams(
            collective_id=0, has_side_effects=True, vmem_limit_bytes=56 * 1024 * 1024),
        cost_estimate=pl.CostEstimate(
            flops=4 * rows * width * ff * 9, bytes_accessed=12 * width * ff, transcendentals=rows * quarter),
    )(tokens, expert_ids.T, gate_codes.T, out_grad, w_in[0], w_out[0])
    out, tgrad, wing, woutg = pl.pallas_call(
        functools.partial(finish, (1, 1, 4, 2)),
        out_shape=shapes,
        in_specs=[hbm] * 4,
        out_specs=(hbm,) * 4,
        scratch_shapes=[pltpu.VMEM(s.shape, BF) for s in shapes] + [pltpu.SemaphoreType.DMA((8,))] * 2,
    )(*results)
    return out, tgrad, wing[None], woutg[None]


def solution(mesh):
    placed = (
        P("expert", "dp"),
        P("expert", None),
        P("expert", None),
        P("expert", "dp"),
        P("expert", "dp", None),
        P("expert", None, "dp"),
    )
    return jax.shard_map(
        body,
        mesh=mesh,
        in_specs=placed,
        out_specs=(
            P("expert", "dp"),
            P("expert", "dp"),
            P("expert", "dp", None),
            P("expert", None, "dp"),
        ),
        check_vma=False,
    )
```

time: 446 us -> 98.4 us (0.22)
  waiting for transfers between devices: 304 us -> 0 us
  Pallas kernels: 0 us -> 97.6 us
  starting transfers between devices: 45 us -> 0 us
  local copies, waits for them, and re-layouts: 32.7 us -> 0 us
  blocking collectives: 25.6 us -> 0 us
  matrix products: 18.7 us -> 0 us
  between operations: 14.6 us -> 0.64 us
    unnamed x6 -> x0, waiting for transfers between devices: 166 us -> none
    all_gather x2 -> x0, waiting for transfers between devices: 105 us -> none  [the longest x1 59.7 us: body(): lax.all_gather((active * up_pre).astype(jnp.bfloat16), 'dp', axis=2, tile...]
    pallas_call x0 -> x2, Pallas kernels: none -> 97.6 us  [the longest x1 95 us: body(): pl.pallas_call(functools.partial(kernel, peers, cap), out_shape=shapes, i...]
    all_to_all x3 -> x0, starting transfers between devices: 44.8 us -> none  [the longest x2 28.1 us: unpack_rows(): lax.all_to_all(shaped, 'expert', split_axis=1, concat_axis=1, tiled=True)]
    all_to_all x3 -> x0, waiting for transfers between devices: 32.8 us -> none  [the longest x1 19.4 us: body(): lax.all_to_all(packed, 'expert', split_axis=1, concat_axis=1, tiled=True)]
    all_to_all x1 -> x0, blocking collectives: 25.6 us -> none  [body(): lax.all_to_all(route_grad, 'expert', split_axis=1, concat_axis=1, tiled=T...]
    dot_general x11 -> x0, matrix products: 18.7 us -> none  [the longest x1 2.88 us: body(): jnp.einsum('lrgf,ldgf->lrd', segment, w_in_split, preferred_element_type=...]
    unnamed x17 -> x0, local copies, waits for them, and re-layouts: 11.7 us -> none
  transfers between devices with their start and end apart: 7 -> 0, of which waited for: 6 -> 0; matrix products, arithmetic and copies ran while one was open for 9% -> 0% of each run, Pallas kernels for 0% -> 0%
where the time goes in v2:
time: 98.4 us; the launch traced here: 98.2 us
  Pallas kernels  97.6 us (99%)
    pallas_call x1, Pallas kernels, body(): pl.pallas_call(functools.partial(kernel, peers, cap), out_shape=shapes, i...  95 us
    pallas_call x1, Pallas kernels, body(): pl.pallas_call(functools.partial(finish, (1, 1, 4, 2)), out_shape=shapes,...  2.61 us

profile of v2, /device:TPU:1, one launch (start us, length us, event | category | flops | bytes accessed | tf_op | source)
XLA Modules:
  0.0 98.2 jit_solution(1512736521248426350)
XLA Ops:
  0.6 95.0 %shard_map.93 = (bf16[128,256]{1,0:T(8,128)(2,1)}, bf16[128,256]{1,0:T(8,128)(2,1)}, bf16[256,3072]{1,0:T(8,128)(2,1)}, bf16[1536,256]{1,0:T(8,128)(2,1)}) custom-call(bf16[128,256]{1,0:T(8,128)(2,1)} %refs_0_.1, s32[8,128]{1,0:T(8,128)} %bitcast.10, s32[8,128]{1,0:T(8,128)} %bitcast.11, bf16[128,256]{1,0:T(8,128)(2,1)} %refs_3_.1, ...), custom_call_target="tpu_custom_call" | custom-call | flops 2717908992 | bytes 4718592 | tf_op jit(solution)/shard_map/pallas_call | solution.py:536
  95.6 2.6 %shard_map.94 = (bf16[128,256]{1,0:T(8,128)(2,1)}, bf16[128,256]{1,0:T(8,128)(2,1)}, bf16[256,3072]{1,0:T(8,128)(2,1)}, bf16[1536,256]{1,0:T(8,128)(2,1)}) custom-call(bf16[128,256]{1,0:T(8,128)(2,1)} %get-tuple-element.12.refs_0_, bf16[128,256]{1,0:T(8,128)(2,1)} %get-tuple-element.13.refs_1_, bf16[256,3072]{1,0:T(8,128)(2,1)} %get-tuple-element.14.refs_2_, ...), custom_call_target="tpu_custom_call" | custom-call | tf_op jit(solution)/shard_map/pallas_call | solution.py:547

commit v3 on v2

--- a/solution.py
+++ b/solution.py
@@ -384,14 +384,12 @@
     hidden = active * up_pre
     hg[0].put(hidden[:, :cut1])
     hg[1].put(hidden[:, cut1:])
+    both(a, "relay", "get2")
     hidden_grad = jnp.concatenate([hg[0].result(), hg[1].result()], axis=1)
     pre[0].put(hidden_grad * up_pre * slopes)
     pre[1].put(hidden_grad * active)
-    both(a, "relay", "get2")
     both(hg, "onward")
     both(pre, "onward")
-    both(hg, "relay", "get2")
-
     flat = lambda ref, where: ref[:, :, where].reshape(rows, -1)
     at = lambda q, chunk, first, width: pl.ds(pl.multiple_of(q * (gathered[chunk].shape[2] // SIDE) + first, LANES), width)
 
@@ -434,10 +432,15 @@
     near_outs = outs(0)
     eo0 = return_outs(0, near_outs)
     ig0 = return_inputs(0, near_outs, inputs(0))
+    both(hg, "relay", "get2")
     both(pre, "relay", "get2")
+
     both(hg, "wait", "get2")
     far_outs = outs(1)
     eo1 = return_outs(1, far_outs)
+
+    both(pre, "wait", "get2")
+    ig1 = return_inputs(1, far_outs, inputs(1))
 
     @pl.loop(0, SIDE)
     def _(q):
@@ -450,8 +453,6 @@
     store_out = pltpu.make_async_copy(woutg, woutg_hbm, local.at[2])
     store_out.start()
 
-    both(pre, "wait", "get2")
-    ig1 = return_inputs(1, far_outs, inputs(1))
 
     for part in range(2):
         @pl.loop(0, SIDE)
@@ -462,14 +463,19 @@
     store_in = pltpu.make_async_copy(wing, wing_hbm, local.at[3])
     store_in.start()
 
+    def parts(table, got, size, chunk):
+        at = pl.ds(chunk * near * size, near * size)
+        rows_ = got[pl.ds(chunk * near, near)].reshape(near * size, LANES)
+        return [dot(table[at, pl.ds(i * LANES, LANES)], rows_, 0, 0) for i in range(4)]
+
     eo0.wait()
+    ig0.wait()
+    ends = parts(back1, e1, one, 0)
+    sides = parts(back2, e2, two, 0)
     eo1.wait()
-    ret2 = e2[...].reshape(peers * two, LANES)
-    sides = [dot(back2[:, pl.ds(i * LANES, LANES)], ret2, 0, 0) for i in range(4)]
-    ig0.wait()
+    sides = [x + y for x, y in zip(sides, parts(back2, e2, two, 1))]
     ig1.wait()
-    ret1 = e1[...].reshape(peers * one, LANES)
-    ends = [dot(back1[:, pl.ds(i * LANES, LANES)], ret1, 0, 0) for i in range(4)]
+    ends = [x + y for x, y in zip(ends, parts(back1, e1, one, 1))]
     out[...] = jnp.concatenate([sides[0] + sides[1], sides[2] + sides[3] + ends[2] + ends[3]], axis=1).astype(BF)
     tgrad[...] = jnp.concatenate([ends[0], ends[1]], axis=1).astype(BF)
     store_out.wait()
@@ -540,7 +546,7 @@
         out_specs=(vmem, vmem, hbm, hbm),
         scratch_shapes=scratch,
         compiler_params=pltpu.CompilerParams(
-            collective_id=0, has_side_effects=True, vmem_limit_bytes=56 * 1024 * 1024),
+            collective_id=0, has_side_effects=True, vmem_limit_bytes=40 * 1024 * 1024),
         cost_estimate=pl.CostEstimate(
             flops=4 * rows * width * ff * 9, bytes_accessed=12 * width * ff, transcendentals=rows * quarter),
     )(tokens, expert_ids.T, gate_codes.T, out_grad, w_in[0], w_out[0])

time: 98.4 us -> 106 us (1.077)
  local copies, waits for them, and re-layouts: 0 us -> 8.82 us
    unnamed x0 -> x20, local copies, waits for them, and re-layouts: none -> 8.82 us
where the time goes in v3:
time: 106 us
  Pallas kernels  96.6 us (91%)
  local copies, waits for them, and re-layouts  8.82 us (8%)
    pallas_call x1, Pallas kernels, body(): pl.pallas_call(functools.partial(kernel, peers, cap), out_shape=shapes, i...  94 us
    unnamed x20, local copies, waits for them, and re-layouts  8.82 us
    pallas_call x1, Pallas kernels, body(): pl.pallas_call(functools.partial(finish, (1, 1, 4, 2)), out_shape=shapes,...  2.6 us

profile of v3, /device:TPU:1, one launch (start us, length us, event | category | flops | bytes accessed | tf_op | source)
XLA Modules:
  0.0 106.0 jit_solution(5795580390633974461)
XLA Ops:
  0.6 0.0 copy-start.4
  0.6 1.4 %copy-done.4 = bf16[1,256,3072]{2,1,0:T(8,128)(2,1)S(1)} copy-done((bf16[1,256,3072]{2,1,0:T(8,128)(2,1)S(1)}, bf16[1,256,3072]{2,1,0:T(8,128)(2,1)}, u32[]{:S(2)}) %copy-start.4) | copy-done | bytes 1572888
  2.0 0.0 copy-start.5
  2.0 1.1 %copy-done.5 = bf16[1,1536,256]{2,1,0:T(8,128)(2,1)S(1)} copy-done((bf16[1,1536,256]{2,1,0:T(8,128)(2,1)S(1)}, bf16[1,1536,256]{2,1,0:T(8,128)(2,1)}, u32[]{:S(2)}) %copy-start.5) | copy-done | bytes 786456
  3.2 0.0 copy-start.6
  3.2 0.8 copy-done.6
  4.0 0.0 copy-start.7
  4.0 0.8 copy-done.7
  4.9 0.0 copy-start.8
  4.9 0.7 copy-done.8
  5.5 0.0 copy-start.9
  5.5 0.7 copy-done.9
  6.2 94.0 %shard_map.93 = (bf16[128,256]{1,0:T(8,128)(2,1)S(1)}, bf16[128,256]{1,0:T(8,128)(2,1)S(1)}, bf16[256,3072]{1,0:T(8,128)(2,1)S(1)}, bf16[1536,256]{1,0:T(8,128)(2,1)S(1)}) custom-call(bf16[128,256]{1,0:T(8,128)(2,1)S(1)} %copy-done.6, s32[8,128]{1,0:T(8,128)S(1)} %bitcast.8, s32[8,128]{1,0:T(8,128)S(1)} %bitcast.9, bf16[128,256]{1,0:T(8,128)(2,1)S(1)} %copy-done.7, ...), custom_call_target="tpu_custom_call" | custom-call | flops 2717908992 | bytes 4718592 | tf_op jit(solution)/shard_map/pallas_call | solution.py:542
  100.2 0.0 copy-start
  100.2 1.1 %copy-done = bf16[256,3072]{1,0:T(8,128)(2,1)} copy-done((bf16[256,3072]{1,0:T(8,128)(2,1)}, bf16[256,3072]{1,0:T(8,128)(2,1)S(1)}, u32[]{:S(2)}) %copy-start) | copy-done | bytes 1572888
  101.3 0.0 copy-start.1
  101.3 0.9 copy-done.1
  102.2 0.0 copy-start.2
  102.2 0.6 copy-done.2
  102.8 0.0 copy-start.3
  102.8 0.6 copy-done.3
  103.4 2.6 %shard_map.94 = (bf16[128,256]{1,0:T(8,128)(2,1)}, bf16[128,256]{1,0:T(8,128)(2,1)}, bf16[256,3072]{1,0:T(8,128)(2,1)}, bf16[1536,256]{1,0:T(8,128)(2,1)}) custom-call(bf16[128,256]{1,0:T(8,128)(2,1)} %copy-done.2, bf16[128,256]{1,0:T(8,128)(2,1)} %copy-done.3, bf16[256,3072]{1,0:T(8,128)(2,1)} %copy-done, bf16[1536,256]{1,0:T(8,128)(2,1)} %copy-done.1), custom_call_target="tpu_custom_call" | custom-call | tf_op jit(solution)/shard_map/pallas_call | solution.py:553
Async XLA Ops:
  0.6 1.4 %copy-start.4 = (bf16[1,256,3072]{2,1,0:T(8,128)(2,1)S(1)}, bf16[1,256,3072]{2,1,0:T(8,128)(2,1)}, u32[]{:S(2)}) copy-start(bf16[1,256,3072]{2,1,0:T(8,128)(2,1)} %param.10) | copy-start | bytes 4718596
  2.0 1.1 %copy-start.5 = (bf16[1,1536,256]{2,1,0:T(8,128)(2,1)S(1)}, bf16[1,1536,256]{2,1,0:T(8,128)(2,1)}, u32[]{:S(2)}) copy-start(bf16[1,1536,256]{2,1,0:T(8,128)(2,1)} %param.11) | copy-start | bytes 2359300
  3.2 0.8 copy-start.6
  4.0 0.8 copy-start.7
  4.9 0.7 copy-start.8
  5.5 0.7 copy-start.9
  100.2 1.2 %copy-start = (bf16[256,3072]{1,0:T(8,128)(2,1)}, bf16[256,3072]{1,0:T(8,128)(2,1)S(1)}, u32[]{:S(2)}) copy-start(bf16[256,3072]{1,0:T(8,128)(2,1)S(1)} %get-tuple-element.14.refs_2_) | copy-start | bytes 4718596
  101.3 0.9 copy-start.1
  102.2 0.6 copy-start.2
  102.8 0.6 copy-start.3
